TPU v7x, 32 devices: a whole 2x2x4 slice. The times are simulated.
32 devices in a mesh: groups: 2 (over y), replica: 4 (over x, core), tensor: 4 (over z).
Axes of the slice: x: 2, y: 2, z: 4, core: 2. Of those that a mesh axis runs over, the one named last changes fastest.
Arguments:
- hidden: bfloat16 [2, 64, 8192], P(None, ('groups', 'replica')), parts along dimension 1, may hold values from -64 to 64
- frozen_query: bfloat16 [2, 64, 8192], P(None, ('groups', 'replica'), 'tensor'), parts along dimension 1, may hold values from -6 to 6
- frozen_key_value: bfloat16 [2, 2, 64, 1024], P(None, None, ('groups', 'replica')), parts along dimension 2, may hold values from -8 to 8
- cache_keys: bfloat16 [64, 64, 512, 128], P(('groups', 'replica'), 'tensor'), parts along dimension 0, may hold values from -12 to 12
- cache_values: bfloat16 [64, 64, 512, 128], P(('groups', 'replica'), 'tensor'), parts along dimension 0, may hold values from -6 to 6
- lengths: int32 [64], P(('groups', 'replica')), parts along dimension 0, may hold values from 128 to 512, as said below
- out_weight: bfloat16 [8192, 8192], P('tensor'), may hold values from -0.75 to 0.75
- down_qkv: bfloat16 [6, 8192, 64], P('groups', 'tensor', 'replica'), parts along dimension 0, may hold values from -0.0625 to 0.0625
- query_up_factor: bfloat16 [128, 8192], P(('groups', 'replica'), 'tensor'), parts along dimension 0, may hold values from -0.75 to 0.75
- key_value_up_factor: bfloat16 [2, 128, 1024], P(None, ('groups', 'replica')), parts along dimension 1, may hold values from -0.75 to 0.75
- output_down_factor: bfloat16 [16384, 64], P(('groups', 'tensor'), 'replica'), parts along dimension 0, may hold values from -0.5 to 0.5
- output_up_factor: bfloat16 [128, 8192], P(('groups', 'replica'), 'tensor'), parts along dimension 0, may hold values from -0.75 to 0.75
- norm_gain: bfloat16 [8192], replicated, may hold values from 0.5 to 1.5
Outputs:
- residual_out: bfloat16 [2, 64, 8192], P(None, ('groups', 'replica'), 'tensor'), parts along dimension 1
- normed_out: bfloat16 [2, 64, 8192], P(None, ('groups', 'replica')), parts along dimension 1
There are 2 independent parts, one for each index of `groups`. A program takes and returns all parts, laid end to end along the dimension named above; an argument that names none is the same for every part. Nothing has to cross between parts.
Inputs may be any that keep to these rules, and one draw needn't show every extreme that they name: `lengths`: some row of the 32 has all 512 slots live.
All inputs are finite; a program needn't handle non-finite values.
Results may differ from a plain program's by a relative error of at most 0.0068.
Values may be sent and summed in bfloat16 or wider, within the bound.
A program may use at most 192 MiB of HBM per device.

v0:
```python
import math

import jax
import jax.numpy as jnp
from jax import lax
from jax.sharding import PartitionSpec as P

HEADS = 64
KV = 8
HD = 128


EPSILON = 1e-06
ADAPTER_SCALING = 0.25
NEG_FILL = -1e30


def rms_scale(values):
    return lax.rsqrt(jnp.mean(values * values, axis=-1, keepdims=True) + EPSILON)


def body(
    hidden,
    frozen_query,
    frozen_key_value,
    cache_keys,
    cache_values,
    lengths,
    out_weight,
    down_qkv,
    query_up_factor,
    key_value_up_factor,
    output_down_factor,
    output_up_factor,
    norm_gain,
):
    tensor_rank = lax.axis_index("tensor")
    tensor_count = lax.axis_size("tensor")
    step_count = hidden.shape[0]
    row_count = hidden.shape[1]
    down_rank, query_up_columns, up_kv_full, output_down_rows, up_o_cols = (
        lax.all_gather(down_qkv, "replica", axis=2, tiled=True),
        lax.all_gather(query_up_factor, "replica", axis=0, tiled=True),
        lax.all_gather(key_value_up_factor, "replica", axis=1, tiled=True),
        lax.all_gather(output_down_factor, "replica", axis=1, tiled=True),
        lax.all_gather(output_up_factor, "replica", axis=0, tiled=True),
    )
    hidden_state = hidden.astype(jnp.float32)
    normed_in = (hidden_state * rms_scale(hidden_state)).astype(jnp.bfloat16)
    share_rows = down_rank.shape[1]
    inputs_part = lax.dynamic_slice_in_dim(normed_in, tensor_rank * share_rows, share_rows, 2)
    partial_rank = jnp.einsum(
        "sbd,pdr->sbpr", inputs_part, down_rank, preferred_element_type=jnp.float32
    )
    rank_sum = lax.psum(partial_rank, "tensor")
    lowrank_activity = rank_sum.astype(jnp.bfloat16)
    heads_here = frozen_query.shape[2] // HD
    query_correction = jnp.einsum(
        "huo,oa->hua",
        lowrank_activity[:, :, 0],
        query_up_columns,
        preferred_element_type=jnp.float32,
    )
    query_vectors = (frozen_query.astype(jnp.float32) + ADAPTER_SCALING * query_correction).astype(
        jnp.bfloat16
    )
    query_vectors = query_vectors.reshape(step_count, row_count, heads_here, HD)
    key_value_correction = jnp.einsum(
        "sbpr,prc->psbc", lowrank_activity[:, :, 1:], up_kv_full, preferred_element_type=jnp.float32
    )
    current_key_value = (
        frozen_key_value.astype(jnp.float32) + ADAPTER_SCALING * key_value_correction
    ).astype(jnp.bfloat16)
    current_key_value = current_key_value.reshape(2, step_count, row_count, KV, HD)
    head_ids = tensor_rank * heads_here + jnp.arange(heads_here)
    selector = (head_ids[:, None] // (HEADS // KV) == jnp.arange(KV)[None, :]).astype(jnp.bfloat16)
    fresh_heads = jnp.einsum(
        "psbgd,hg->psbhd", current_key_value, selector, preferred_element_type=jnp.float32
    ).astype(jnp.bfloat16)
    appended_keys = fresh_heads[0]
    appended_values = fresh_heads[1]
    slot_count = cache_keys.shape[2]
    cache_scores = jnp.einsum(
        "sbhd,bhpd->sbhp", query_vectors, cache_keys, preferred_element_type=jnp.float32
    ) / math.sqrt(HD)
    visible = jnp.arange(slot_count)[None, None, None, :] < lengths[None, :, None, None]
    cache_scores = jnp.where(visible, cache_scores, NEG_FILL)
    fresh_scores = jnp.einsum(
        "sbhd,tbhd->sbht", query_vectors, appended_keys, preferred_element_type=jnp.float32
    ) / math.sqrt(HD)
    causal = jnp.arange(step_count)[None, :] <= jnp.arange(step_count)[:, None]
    fresh_scores = jnp.where(causal[:, None, None, :], fresh_scores, NEG_FILL)
    highest = jnp.maximum(jnp.max(cache_scores, axis=-1), jnp.max(fresh_scores, axis=-1))[..., None]
    cache_exp = jnp.exp(cache_scores - highest)
    fresh_exp = jnp.exp(fresh_scores - highest)
    denominator = jnp.sum(cache_exp, axis=-1, keepdims=True) + jnp.sum(
        fresh_exp, axis=-1, keepdims=True
    )
    cache_weights = (cache_exp / denominator).astype(jnp.bfloat16)
    fresh_weights = (fresh_exp / denominator).astype(jnp.bfloat16)
    mixed = jnp.einsum(
        "sbhp,bhpd->sbhd", cache_weights, cache_values, preferred_element_type=jnp.float32
    )
    mixed = mixed + jnp.einsum(
        "sbht,tbhd->sbhd", fresh_weights, appended_values, preferred_element_type=jnp.float32
    )
    attention_result = mixed.astype(jnp.bfloat16).reshape(step_count, row_count, heads_here * HD)
    base_part = jnp.einsum(
        "sbc,cd->sbd", attention_result, out_weight, preferred_element_type=jnp.float32
    )
    lowrank_portion = jnp.einsum(
        "njk,ko->njo", attention_result, output_down_rows, preferred_element_type=jnp.float32
    )
    output_up_complete = lax.all_gather(up_o_cols, "tensor", axis=1, tiled=True)
    frozen_total_sum, lowrank_output = lax.psum((base_part, lowrank_portion), "tensor")
    widened_heads = jnp.einsum(
        "hwt,tm->hwm",
        lowrank_output,
        output_up_complete.astype(jnp.float32),
        precision=lax.Precision.HIGHEST,
    )
    refreshed_state = hidden_state + (frozen_total_sum + ADAPTER_SCALING * widened_heads)
    normed_out = (
        refreshed_state * rms_scale(refreshed_state) * norm_gain.astype(jnp.float32)
    ).astype(jnp.bfloat16)
    share_width = refreshed_state.shape[2] // tensor_count
    residual_out = lax.dynamic_slice_in_dim(
        refreshed_state, tensor_rank * share_width, share_width, 2
    ).astype(jnp.bfloat16)
    return (residual_out, normed_out)


def solution(mesh):
    in_specs = (
        P(None, ("groups", "replica"), None),
        P(None, ("groups", "replica"), "tensor"),
        P(None, None, ("groups", "replica"), None),
        P(("groups", "replica"), "tensor", None, None),
        P(("groups", "replica"), "tensor", None, None),
        P(("groups", "replica")),
        P("tensor", None),
        P("groups", "tensor", "replica"),
        P(("groups", "replica"), "tensor"),
        P(None, ("groups", "replica"), None),
        P(("groups", "tensor"), "replica"),
        P(("groups", "replica"), "tensor"),
        P(),
    )
    out_specs = (P(None, ("groups", "replica"), "tensor"), P(None, ("groups", "replica"), None))
    return jax.shard_map(body, mesh=mesh, in_specs=in_specs, out_specs=out_specs, check_vma=False)
```

profile of v0, /device:TPU:0, one launch (start us, length us, event | category | flops | bytes accessed | tf_op | source)
XLA Modules:
  0.0 164.3 jit_solution(14229053956330666822)
XLA Ops:
  7.2 1.0 convert_element_type.47
  8.2 1.1 multiply_reduce_fusion.1
  9.3 10.2 %all_gather.18 = bf16[3,2048,64]{1,2,0:T(8,128)(2,1)S(1)} all-gather(bf16[3,2048,16]{1,2,0:T(8,128)(2,1)} %param.20), channel_id=1, replica_groups=mesh['groups'=2,'replica'=4,'tensor'=4] {'replica'}, dimensions={2}, use_global_device_ids=true | all-gather | bytes 983040 | tf_op jit(solution)/shard_map/all_gather | solution.py:42
  19.6 0.4 fusion.14
  20.0 19.2 %psum.21 = bf16[2,8,3,64]{3,1,2,0:T(8,128)(2,1)S(1)} all-reduce(f32[2,8,3,64]{3,1,2,0:T(8,128)S(1)} %fusion.14), channel_id=1, replica_groups=mesh['groups'=2,'replica'=4,'tensor'=4] {'tensor'}, use_global_device_ids=true, to_apply=%region_1.0 | all-reduce | flops 3072 | bytes 18432 | tf_op jit(solution)/shard_map/psum | solution.py:55
  39.2 6.0 %all_gather.20 = bf16[2,64,1024]{2,1,0:T(8,128)(2,1)S(1)} all-gather(bf16[2,16,1024]{2,1,0:T(8,128)(2,1)} %param.22), channel_id=1, replica_groups=mesh['groups'=2,'replica'=4,'tensor'=4] {'replica'}, dimensions={1}, use_global_device_ids=true | all-gather | bytes 327680 | tf_op jit(solution)/shard_map/all_gather | solution.py:44
  45.2 1.0 fusion.11
  46.5 6.1 %all_gather.19 = bf16[64,2048]{1,0:T(8,128)(2,1)S(1)} all-gather(bf16[16,2048]{1,0:T(8,128)(2,1)} %param.21), channel_id=1, replica_groups=mesh['groups'=2,'replica'=4,'tensor'=4] {'replica'}, dimensions={0}, use_global_device_ids=true | all-gather | bytes 327680 | tf_op jit(solution)/shard_map/all_gather | solution.py:43
  52.5 1.0 fusion.12
  53.5 0.3 fusion.32
  54.2 0.7 iota_compare_fusion
  54.9 10.3 %fusion.43 = (f32[2,8,16]{0,2,1:T(8,128)S(1)}, f32[2,8,16,512]{3,0,2,1:T(2,128)S(1)}) fusion(bf16[8,16,512,128]{3,2,1,0:T(8,128)(2,1)} %param.16, bf16[2,8,16,128]{3,1,2,0:T(8,128)(2,1)S(1)} %fusion.12, pred[8,512]{1,0:T(8,128)(4,1)S(1)} %iota_compare_fusion), kind=kOutput, calls=%fused_computation.69 | convolution fusion | flops 33947392 | bytes 17372160 | tf_op jit(solution)/shard_map/sbhd,bhpd->sbhp/dot_general | solution.py:83
  65.6 0.7 fusion.16
  66.4 7.2 %fusion.17 = f32[8,16,2,128]{3,2,1,0:T(2,128)S(1)} fusion(bf16[8,16,512,128]{3,2,1,0:T(8,128)(2,1)} %param.17, f32[2,8,16,512]{3,0,2,1:T(2,128)S(1)} %get-tuple-element.5, f32[2,8,16]{0,2,1:T(8,128)S(1)} %add.71, f32[2,8,16]{0,2,1:T(8,128)S(1)} %max.7), kind=kOutput, calls=%fused_computation.27 | convolution fusion | flops 33947648 | bytes 17434624 | tf_op jit(solution)/shard_map/sbhp,bhpd->sbhd/dot_general | solution.py:101
  73.8 0.3 fusion.30
  74.2 13.7 %fusion = f32[2,8,8192]{2,1,0:T(8,128)} fusion(bf16[2,8,2048]{2,1,0:T(8,128)(2,1)S(1)} %reshape.113, bf16[2048,8192]{1,0:T(8,128)(2,1)} %param.19), kind=kOutput, calls=%fused_computation | convolution fusion | flops 536870912 | bytes 34144256 | tf_op jit(solution)/shard_map/sbc,cd->sbd/dot_general | solution.py:108
  88.0 6.3 %all_gather.22 = bf16[64,2048]{1,0:T(8,128)(2,1)} all-gather(bf16[16,2048]{1,0:T(8,128)(2,1)S(1)} %copy-done.1), channel_id=1, replica_groups=mesh['groups'=2,'replica'=4,'tensor'=4] {'replica'}, dimensions={0}, use_global_device_ids=true | all-gather | bytes 327680 | tf_op jit(solution)/shard_map/all_gather | solution.py:46
  94.4 5.9 %all_gather.21 = bf16[2048,64]{0,1:T(8,128)(2,1)S(1)} all-gather(bf16[2048,16]{0,1:T(8,128)(2,1)S(1)} %copy-done.2), channel_id=1, replica_groups=mesh['groups'=2,'replica'=4,'tensor'=4] {'replica'}, dimensions={1}, use_global_device_ids=true | all-gather | bytes 327680 | tf_op jit(solution)/shard_map/all_gather | solution.py:45
  100.4 8.6 %psum.23 = f32[2,8,64]{2,1,0:T(8,128)S(1)} all-reduce(f32[2,8,64]{2,1,0:T(8,128)S(1)} %fusion.19), channel_id=1, replica_groups=mesh['groups'=2,'replica'=4,'tensor'=4] {'tensor'}, use_global_device_ids=true, to_apply=%region_7.8 | all-reduce | flops 1024 | bytes 8192 | tf_op jit(solution)/shard_map/psum | solution.py:115
  109.0 15.4 %all-reduce.2.cloned.1.call-done = f32[2,8,8192]{2,1,0:T(8,128)} async-done(((f32[2,8,8192]{2,1,0:T(8,128)}), f32[2,8,8192]{2,1,0:T(8,128)}) %all-reduce.2.cloned.1.call-update) | async-done | bytes 524304 | tf_op jit(solution)/shard_map/psum | solution.py:115
  124.4 29.5 %all-gather.2.cloned.1.call-done = bf16[64,8192]{1,0:T(8,128)(2,1)} async-done(((bf16[64,2048]{1,0:T(8,128)(2,1)}), bf16[64,8192]{1,0:T(8,128)(2,1)}) %all-gather.2.cloned.1.call-update) | async-done | bytes 1048592 | tf_op jit(solution)/shard_map/all_gather | solution.py:114
  154.0 2.0 %multiply_reduce_fusion = (f32[2,8]{1,0:T(2,128)S(1)}, f32[2,8,8192]{2,1,0:T(8,128)S(1)}) fusion(f32[2,8,8192]{2,1,0:T(8,128)} %all-reduce.2.cloned.1.call-done, f32[2,8,64]{2,1,0:T(8,128)S(1)} %psum.23, bf16[64,8192]{1,0:T(8,128)(2,1)} %all-gather.2.cloned.1.call-done, bf16[2,8,8192]{2,1,0:T(8,128)(2,1)S(1)} %copy-done), kind=kOutput, calls=%fused_computation.22 | convolution fusion | flops 101449712 | bytes 2363456 | tf_op jit(solution)/shard_map/hwt,tm->hwm/dot_general | solution.py:116
  156.0 0.6 dynamic-slice_convert_fusion
  156.6 0.8 multiply_convert_fusion
  (33 shorter events, 1.7 us)
Async XLA Ops:
  7.2 117.3 %all-reduce.2.cloned.1.call-start = ((), (), s32[]{:S(2)}) async-start(), calls=%async_computation | async-start | bytes 1048576 | tf_op jit(solution)/shard_map/psum | solution.py:115
  74.2 13.8 %copy-start.1 = (bf16[16,2048]{1,0:T(8,128)(2,1)S(1)}, bf16[16,2048]{1,0:T(8,128)(2,1)}, u32[]{:S(2)}) copy-start(bf16[16,2048]{1,0:T(8,128)(2,1)} %param.24) | copy-start | bytes 196612
  74.2 20.2 %copy-start.3 = (bf16[8192]{0:T(1024)(128)(2,1)S(1)}, bf16[8192]{0:T(1024)(128)(2,1)}, u32[]{:S(2)}) copy-start(bf16[8192]{0:T(1024)(128)(2,1)} %param.25) | copy-start | bytes 49156
  74.2 20.2 %copy-start.2 = (bf16[2048,16]{0,1:T(8,128)(2,1)S(1)}, bf16[2048,16]{0,1:T(8,128)(2,1)}, u32[]{:S(2)}) copy-start(bf16[2048,16]{0,1:T(8,128)(2,1)} %param.23) | copy-start | bytes 196612
  74.2 79.7 %copy-start = (bf16[2,8,8192]{2,1,0:T(8,128)(2,1)S(1)}, bf16[2,8,8192]{2,1,0:T(8,128)(2,1)}, u32[]{:S(2)}) copy-start(bf16[2,8,8192]{2,1,0:T(8,128)(2,1)} %param.13) | copy-start | bytes 786436
  88.0 66.0 %all-gather.2.cloned.1.call-start = ((), (), s32[]{:S(2)}) async-start(), calls=%async_computation.1 | async-start | bytes 1310720 | tf_op jit(solution)/shard_map/all_gather | solution.py:114
Sparse Core Ops, SparseCore 0:
  88.1 36.3 all-reduce.1
  126.0 27.9 all-gather.1
where the time goes:
time: 165 us; the launch traced here: 164 us
  blocking collectives  62.3 us (38%)
  waiting for transfers between devices  45 us (27%)
  matrix products  36.5 us (22%)
  between operations  14.2 us (9%)
  other arithmetic  4.68 us (3%)
    all_gather x1, waiting for transfers between devices, body(): output_up_complete = lax.all_gather(up_o_cols, 'tensor', axis=1, tiled=True)  29.5 us
    psum x1, blocking collectives, body(): rank_sum = lax.psum(partial_rank, 'tensor')  19.2 us
    psum x1, waiting for transfers between devices, body(): lax.psum((base_part, lowrank_portion), 'tensor')  15.4 us
    dot_general x1, matrix products, body(): jnp.einsum('sbc,cd->sbd', attention_result, out_weight, preferred_element...  13.7 us
    dot_general x1, matrix products, body(): jnp.einsum('sbhd,bhpd->sbhp', query_vectors, cache_keys, preferred_elemen...  10.3 us
    all_gather x1, blocking collectives, body(): lax.all_gather(down_qkv, 'replica', axis=2, tiled=True)  10.2 us
    psum x1, blocking collectives, body(): lax.psum((base_part, lowrank_portion), 'tensor')  8.59 us
    dot_general x1, matrix products, body(): jnp.einsum('sbhp,bhpd->sbhd', cache_weights, cache_values, preferred_elem...  7.15 us
  transfers between devices with their start and end apart: 2, of which 2 were waited for; matrix products, arithmetic and copies ran while one was open for 0% of the time, Pallas kernels for 0%

commit v1 on v0

--- a/solution.py
+++ b/solution.py
@@ -1,8 +1,11 @@
+import functools
 import math
 
 import jax
 import jax.numpy as jnp
 from jax import lax
+from jax.experimental import pallas as pl
+from jax.experimental.pallas import tpu as pltpu
 from jax.sharding import PartitionSpec as P
 
 HEADS = 64
@@ -130,6 +133,497 @@
     return (residual_out, normed_out)
 
 
+BLOCK = 512
+SLOTS = 8
+MESH = pl.DeviceIdType.MESH
+
+
+def fits(mesh):
+    return KV % mesh.shape["tensor"] == 0
+
+
+def dot_nt(a, b):
+    return lax.dot_general(a, b, (((1,), (1,)), ((), ())), preferred_element_type=jnp.float32)
+
+
+def fused_kernel(
+    steps,
+    replicas,
+    shards,
+    hid,
+    frozen_q,
+    frozen_kv,
+    lens,
+    up_q,
+    up_kv,
+    up_o,
+    gain,
+    down_hbm,
+    down_o_hbm,
+    keys_hbm,
+    values_hbm,
+    weight_hbm,
+    res_out,
+    norm_out,
+    keys,
+    values,
+    wbuf,
+    down,
+    down_o,
+    hid_all,
+    up_q_all,
+    up_kv_all,
+    up_o_all,
+    down_o_all,
+    part,
+    part_all,
+    q_heads,
+    k_heads,
+    v_heads,
+    att_heads,
+    sums_out,
+    sums_in,
+    own,
+    rank_out,
+    full,
+    kv_sem,
+    w_sem,
+    down_sem,
+    rep_send,
+    rep_recv,
+    part_send,
+    part_recv,
+    sum_send,
+    sum_recv,
+    rank_send,
+    rank_recv,
+    full_send,
+    full_recv,
+):
+    me_r = lax.axis_index("replica")
+    me_t = lax.axis_index("tensor")
+    tokens, width = hid.shape
+    rows = tokens // steps
+    share = width // shards
+    chunks = share // BLOCK
+    heads = keys.shape[1]
+    slots = keys.shape[2]
+    rank_share = up_q.shape[0]
+    kv_width = up_kv_all.shape[3]
+    depth = hid_all.shape[2]
+
+    def key_copy(b):
+        return pltpu.make_async_copy(keys_hbm.at[b], keys.at[b], kv_sem.at[0, b])
+
+    def value_copy(b):
+        return pltpu.make_async_copy(values_hbm.at[b], values.at[b], kv_sem.at[1, b])
+
+    def weight_copy(m, c, slot):
+        column = pl.multiple_of(lax.rem(me_t + m, shards) * share + c * BLOCK, BLOCK)
+        return pltpu.make_async_copy(
+            weight_hbm.at[:, pl.ds(column, BLOCK)], wbuf.at[slot], w_sem.at[slot]
+        )
+
+    down_copy = pltpu.make_async_copy(down_hbm, down, down_sem.at[0])
+    down_o_copy = pltpu.make_async_copy(down_o_hbm, down_o, down_sem.at[1])
+    down_copy.start()
+    down_o_copy.start()
+
+    @pl.loop(0, rows)
+    def _(b):
+        key_copy(b).start()
+        value_copy(b).start()
+
+    order = [m % shards for m in range(1, shards + 1)]
+    held = SLOTS // chunks
+    for place in range(min(held, shards)):
+
+        @pl.loop(0, chunks)
+        def _(c, place=place):
+            weight_copy(order[place], c, place * chunks + c).start()
+
+    barrier = pltpu.get_barrier_semaphore()
+    for k in range(replicas):
+        for m in range(shards):
+            if k or m:
+                pl.semaphore_signal(
+                    barrier,
+                    inc=1,
+                    device_id={
+                        "replica": lax.rem(me_r + k, replicas),
+                        "tensor": lax.rem(me_t + m, shards),
+                    },
+                    device_id_type=MESH,
+                )
+    pl.semaphore_wait(barrier, replicas * shards - 1)
+
+    def to_replica(src, dst, what, k):
+        return pltpu.make_async_remote_copy(
+            src_ref=src,
+            dst_ref=dst.at[k],
+            send_sem=rep_send.at[what, k],
+            recv_sem=rep_recv.at[what, k],
+            device_id={"replica": lax.rem(me_r + k, replicas)},
+            device_id_type=MESH,
+        )
+
+    def to_shard(src, dst, send, recv, m):
+        return pltpu.make_async_remote_copy(
+            src_ref=src,
+            dst_ref=dst,
+            send_sem=send,
+            recv_sem=recv,
+            device_id={"tensor": lax.rem(me_t + m, shards)},
+            device_id_type=MESH,
+        )
+
+    hid_mine = hid.at[:, pl.ds(pl.multiple_of(me_t * depth, 128), depth)]
+    kv_mine = up_kv.at[:, :, pl.ds(pl.multiple_of(me_t * kv_width, 128), kv_width)]
+    hid_copies = [to_replica(hid_mine, hid_all, 0, k) for k in range(1, replicas)]
+    up_q_copies = [to_replica(up_q, up_q_all, 1, k) for k in range(1, replicas)]
+    up_kv_copies = [to_replica(kv_mine, up_kv_all, 2, k) for k in range(1, replicas)]
+    up_o_copies = [to_replica(up_o, up_o_all, 3, k) for k in range(1, replicas)]
+    for copy in hid_copies + up_q_copies + up_kv_copies:
+        copy.start()
+    hid_all[0] = hid_mine[...]
+    up_q_all[0] = up_q[...]
+    up_kv_all[0] = kv_mine[...]
+    up_o_all[0] = up_o[...]
+
+    state = hid[...].astype(jnp.float32)
+    scale = lax.rsqrt(jnp.mean(state * state, axis=-1, keepdims=True) + EPSILON)
+
+    down_copy.wait()
+    for copy in hid_copies:
+        copy.wait_recv()
+    hid_rows = hid_all[...].reshape(replicas * tokens, depth)
+    pieces = [
+        jnp.dot(hid_rows, down[p], preferred_element_type=jnp.float32) for p in range(3)
+    ]
+    pieces.append(jnp.zeros((replicas * tokens, 128 - 3 * rank_share), jnp.float32))
+    part[...] = jnp.concatenate(pieces, axis=1).reshape(replicas, tokens, 128)
+    part_copies = []
+    for k in range(replicas):
+        for m in range(shards):
+            if k or m:
+                back = (replicas - k) % replicas
+                part_copies.append(
+                    pltpu.make_async_remote_copy(
+                        src_ref=part.at[k],
+                        dst_ref=part_all.at[back, m],
+                        send_sem=part_send.at[back, m],
+                        recv_sem=part_recv.at[back, m],
+                        device_id={
+                            "replica": lax.rem(me_r + back, replicas),
+                            "tensor": lax.rem(me_t + m, shards),
+                        },
+                        device_id_type=MESH,
+                    )
+                )
+                part_copies[-1].start()
+    part_all[0, 0] = part[0]
+
+    down_o_copy.wait()
+    eye = jnp.where(
+        lax.broadcasted_iota(jnp.int32, (rank_share, rank_share), 0)
+        == lax.broadcasted_iota(jnp.int32, (rank_share, rank_share), 1),
+        1.0,
+        0.0,
+    ).astype(jnp.bfloat16)
+    down_o_all[0] = dot_nt(eye, down_o[...]).astype(jnp.bfloat16)
+    down_o_copies = [
+        to_replica(down_o_all.at[0], down_o_all, 4, k) for k in range(1, replicas)
+    ]
+    for copy in down_o_copies + up_o_copies:
+        copy.start()
+
+    for copy in part_copies:
+        copy.wait_recv()
+    ranks = []
+    for k in range(replicas):
+        total = part_all[k, 0]
+        for m in range(1, shards):
+            total = total + part_all[k, m]
+        ranks.append((total * scale).astype(jnp.bfloat16))
+
+    def rank_of(p):
+        return jnp.concatenate(
+            [r[:, p * rank_share : (p + 1) * rank_share] for r in ranks], axis=1
+        )
+
+    for copy in up_q_copies + up_kv_copies:
+        copy.wait_recv()
+    queries = frozen_q[...].astype(jnp.float32) + ADAPTER_SCALING * jnp.dot(
+        rank_of(0),
+        up_q_all[...].reshape(replicas * rank_share, up_q.shape[1]),
+        preferred_element_type=jnp.float32,
+    )
+    queries = queries.astype(jnp.bfloat16).astype(jnp.float32)
+    for h in range(heads):
+        q_heads[h] = queries[:, h * HD : (h + 1) * HD]
+    group = HEADS // KV
+    kv_columns = pl.ds(pl.multiple_of(me_t * kv_width, 128), kv_width)
+    for p, target in ((0, k_heads), (1, v_heads)):
+        up = jnp.concatenate([up_kv_all[k, p] for k in range(replicas)], axis=0)
+        fresh = frozen_kv[p, :, kv_columns].astype(jnp.float32) + ADAPTER_SCALING * jnp.dot(
+            rank_of(1 + p), up, preferred_element_type=jnp.float32
+        )
+        fresh = fresh.astype(jnp.bfloat16).astype(jnp.float32)
+        for h in range(heads):
+            g = h // group
+            target[h] = fresh[:, g * HD : (g + 1) * HD]
+
+    lines = steps * heads
+    line_head = lax.rem(lax.broadcasted_iota(jnp.int32, (lines, HD), 0), heads)
+    line_step = lax.broadcasted_iota(jnp.int32, (lines, 1), 0) // heads
+    place = lax.broadcasted_iota(jnp.int32, (lines, slots), 1)
+    root = 1.0 / math.sqrt(HD)
+
+    @pl.loop(0, rows)
+    def _(b):
+        key_copy(b).wait()
+        value_copy(b).wait()
+
+        def line(source, s):
+            return source[:, pl.ds(s * rows + b, 1), :].reshape(heads, HD)
+
+        query = jnp.concatenate([line(q_heads, s) for s in range(steps)], axis=0)
+        scores = jnp.zeros((lines, slots), jnp.float32)
+        for h in range(0, heads, 2):
+            left = jnp.concatenate(
+                [jnp.where(line_head == h + i, query, 0.0) for i in range(2)], axis=1
+            ).astype(jnp.bfloat16)
+            pair = jnp.concatenate([keys[b, h], keys[b, h + 1]], axis=1)
+            scores = scores + dot_nt(left, pair)
+        scores = jnp.where(place < lens[b], scores * root, NEG_FILL)
+        highest = jnp.max(scores, axis=-1, keepdims=True)
+        fresh_scores = []
+        for t in range(steps):
+            new_key = jnp.concatenate([line(k_heads, t)] * steps, axis=0)
+            score = jnp.sum(query * new_key, axis=-1, keepdims=True) * root
+            score = jnp.where(line_step >= t, score, NEG_FILL)
+            fresh_scores.append(score)
+            highest = jnp.maximum(highest, score)
+        weights = jnp.exp(scores - highest)
+        total = jnp.sum(weights, axis=-1, keepdims=True)
+        fresh_exp = [jnp.exp(score - highest) for score in fresh_scores]
+        for value in fresh_exp:
+            total = total + value
+        inverse = 1.0 / total
+        probs = (weights * inverse).astype(jnp.bfloat16)
+        mixed = jnp.zeros((lines, HD), jnp.float32)
+        for t in range(steps):
+            new_value = jnp.concatenate([line(v_heads, t)] * steps, axis=0)
+            prob = (fresh_exp[t] * inverse).astype(jnp.bfloat16).astype(jnp.float32)
+            mixed = mixed + prob * new_value
+        for h in range(0, heads, 2):
+            pair = jnp.concatenate([values[b, h], values[b, h + 1]], axis=1)
+            both = jnp.dot(probs, pair, preferred_element_type=jnp.float32)
+            for i in range(2):
+                mixed = mixed + jnp.where(
+                    line_head == h + i, both[:, i * HD : (i + 1) * HD], 0.0
+                )
+        for s in range(steps):
+            att_heads[:, pl.ds(s * rows + b, 1), :] = mixed[
+                s * heads : (s + 1) * heads
+            ].reshape(heads, 1, HD)
+
+    attended = jnp.concatenate([att_heads[h] for h in range(heads)], axis=1).astype(jnp.bfloat16)
+
+    for copy in down_o_copies:
+        copy.wait_recv()
+    low = dot_nt(attended, down_o_all[...].reshape(replicas * rank_share, depth))
+    rank_total = replicas * rank_share
+    rank_out[0] = jnp.concatenate(
+        [low, jnp.zeros((tokens, 128 - rank_total), jnp.float32)], axis=1
+    )
+    rank_copies = [
+        to_shard(rank_out.at[0], rank_out.at[m], rank_send.at[m], rank_recv.at[m], m)
+        for m in range(1, shards)
+    ]
+    for copy in rank_copies:
+        copy.start()
+
+    def sum_copy(m, c):
+        return to_shard(
+            sums_out.at[m, c], sums_in.at[m, c], sum_send.at[m, c], sum_recv.at[m, c], m
+        )
+
+    for spot, m in enumerate(order):
+        base = (spot % held) * chunks
+
+        @pl.loop(0, chunks)
+        def _(c, m=m, spot=spot, base=base):
+            weight_copy(m, c, base + c).wait()
+            product = jnp.dot(attended, wbuf[base + c], preferred_element_type=jnp.float32)
+            if m:
+                sums_out[m, c] = product.astype(jnp.bfloat16)
+                sum_copy(m, c).start()
+            else:
+                own[c] = product
+            if spot + held < shards:
+                weight_copy(order[spot + held], c, base + c).start()
+
+    for copy in rank_copies + up_o_copies:
+        copy.wait_recv()
+    rank_sum = rank_out[0]
+    for m in range(1, shards):
+        rank_sum = rank_sum + rank_out[m]
+    rank_sum = rank_sum[:, :rank_total] * ADAPTER_SCALING
+    rank_high = rank_sum.astype(jnp.bfloat16)
+    rank_low = (rank_sum - rank_high.astype(jnp.float32)).astype(jnp.bfloat16)
+
+    def full_copy(m, c):
+        spot = me_t * chunks + c
+        return to_shard(
+            full.at[spot], full.at[spot], full_send.at[m, c], full_recv.at[m, c], m
+        )
+
+    for c in range(chunks):
+        columns = slice(c * BLOCK, (c + 1) * BLOCK)
+        up = jnp.concatenate([up_o_all[k, :, columns] for k in range(replicas)], axis=0)
+        updated = jnp.dot(rank_high, up, preferred_element_type=jnp.float32) + jnp.dot(
+            rank_low, up, preferred_element_type=jnp.float32
+        )
+        mine = pl.ds(pl.multiple_of(me_t * share + c * BLOCK, BLOCK), BLOCK)
+        updated = updated + own[c] + hid[:, mine].astype(jnp.float32)
+        for m in range(1, shards):
+            sum_copy(m, c).wait_recv()
+            updated = updated + sums_in[m, c].astype(jnp.float32)
+        rounded = updated.astype(jnp.bfloat16)
+        res_out[:, columns] = rounded
+        full[me_t * chunks + c] = rounded
+        for m in range(1, shards):
+            full_copy(m, c).start()
+
+    def arrived(m, c):
+        spot = lax.rem(me_t + shards - m, shards) * chunks + c
+        return to_shard(
+            full.at[spot], full.at[spot], full_send.at[m, c], full_recv.at[m, c], m
+        )
+
+    for c in range(chunks):
+        for m in range(1, shards):
+            arrived(m, c).wait_recv()
+    square = jnp.zeros((tokens, BLOCK), jnp.float32)
+    for i in range(shards * chunks):
+        block = full[i].astype(jnp.float32)
+        square = square + block * block
+    norm = lax.rsqrt(jnp.sum(square, axis=-1, keepdims=True) / width + EPSILON)
+    for i in range(shards * chunks):
+        columns = slice(i * BLOCK, (i + 1) * BLOCK)
+        norm_out[:, columns] = (
+            full[i].astype(jnp.float32) * norm * gain[:, columns].astype(jnp.float32)
+        ).astype(jnp.bfloat16)
+
+    for copy in (
+        hid_copies + up_q_copies + up_kv_copies + up_o_copies + down_o_copies + part_copies
+    ):
+        copy.wait_send()
+    for copy in rank_copies:
+        copy.wait_send()
+    for m in range(1, shards):
+        for c in range(chunks):
+            sum_copy(m, c).wait_send()
+            full_copy(m, c).wait_send()
+
+
+def body_fused(
+    hidden,
+    frozen_query,
+    frozen_key_value,
+    cache_keys,
+    cache_values,
+    lengths,
+    out_weight,
+    down_qkv,
+    query_up_factor,
+    key_value_up_factor,
+    output_down_factor,
+    output_up_factor,
+    norm_gain,
+):
+    replicas = lax.axis_size("replica")
+    shards = lax.axis_size("tensor")
+    steps, rows, width = hidden.shape
+    tokens = steps * rows
+    share = width // shards
+    chunks = share // BLOCK
+    head_count = cache_keys.shape[1]
+    depth = out_weight.shape[0]
+    rank_share = query_up_factor.shape[0]
+    kv_width = key_value_up_factor.shape[2] // shards
+    vmem = pl.BlockSpec(memory_space=pltpu.VMEM)
+    smem = pl.BlockSpec(memory_space=pltpu.SMEM)
+    hbm = pl.BlockSpec(memory_space=pl.ANY)
+    bf16, f32 = jnp.bfloat16, jnp.float32
+    dma = pltpu.SemaphoreType.DMA
+    per_head = pltpu.VMEM((head_count, tokens, HD), f32)
+    residual, normed = pl.pallas_call(
+        functools.partial(fused_kernel, steps, replicas, shards),
+        out_shape=(
+            jax.ShapeDtypeStruct((tokens, share), bf16),
+            jax.ShapeDtypeStruct((tokens, width), bf16),
+        ),
+        in_specs=[vmem] * 3 + [smem] + [vmem] * 4 + [hbm] * 5,
+        out_specs=(vmem, vmem),
+        scratch_shapes=[
+            pltpu.VMEM(cache_keys.shape, bf16),
+            pltpu.VMEM(cache_values.shape, bf16),
+            pltpu.VMEM((SLOTS, depth, BLOCK), bf16),
+            pltpu.VMEM(down_qkv.shape, bf16),
+            pltpu.VMEM(output_down_factor.shape, bf16),
+            pltpu.VMEM((replicas, tokens, depth), bf16),
+            pltpu.VMEM((replicas, rank_share, depth), bf16),
+            pltpu.VMEM((replicas, 2, rank_share, kv_width), bf16),
+            pltpu.VMEM((replicas, rank_share, share), bf16),
+            pltpu.VMEM((replicas, rank_share, depth), bf16),
+            pltpu.VMEM((replicas, tokens, 128), f32),
+            pltpu.VMEM((replicas, shards, tokens, 128), f32),
+            per_head,
+            per_head,
+            per_head,
+            per_head,
+            pltpu.VMEM((shards, chunks, tokens, BLOCK), bf16),
+            pltpu.VMEM((shards, chunks, tokens, BLOCK), bf16),
+            pltpu.VMEM((chunks, tokens, BLOCK), f32),
+            pltpu.VMEM((shards, tokens, 128), f32),
+            pltpu.VMEM((shards * chunks, tokens, BLOCK), bf16),
+            dma((2, rows)),
+            dma((SLOTS,)),
+            dma((2,)),
+            dma((5, replicas)),
+            dma((5, replicas)),
+            dma((replicas, shards)),
+            dma((replicas, shards)),
+            dma((shards, chunks)),
+            dma((shards, chunks)),
+            dma((shards,)),
+            dma((shards,)),
+            dma((shards, chunks)),
+            dma((shards, chunks)),
+        ],
+        compiler_params=pltpu.CompilerParams(
+            collective_id=0, has_side_effects=True, vmem_limit_bytes=62 * 2**20
+        ),
+    )(
+        hidden.reshape(tokens, width),
+        frozen_query.reshape(tokens, frozen_query.shape[2]),
+        frozen_key_value.reshape(2, tokens, frozen_key_value.shape[3]),
+        lengths,
+        query_up_factor,
+        key_value_up_factor,
+        output_up_factor,
+        norm_gain.reshape(1, width),
+        down_qkv,
+        output_down_factor,
+        cache_keys,
+        cache_values,
+        out_weight,
+    )
+    return residual.reshape(steps, rows, share), normed.reshape(steps, rows, width)
+
+
 def solution(mesh):
     in_specs = (
         P(None, ("groups", "replica"), None),
@@ -147,4 +641,5 @@
         P(),
     )
     out_specs = (P(None, ("groups", "replica"), "tensor"), P(None, ("groups", "replica"), None))
-    return jax.shard_map(body, mesh=mesh, in_specs=in_specs, out_specs=out_specs, check_vma=False)
+    chosen = body_fused if fits(mesh) else body
+    return jax.shard_map(chosen, mesh=mesh, in_specs=in_specs, out_specs=out_specs, check_vma=False)

time: 165 us -> 55.2 us (0.33)
  blocking collectives: 62.3 us -> 0 us
  Pallas kernels: 0 us -> 45.5 us
  waiting for transfers between devices: 45 us -> 0 us
  matrix products: 36.5 us -> 0 us
  between operations: 14.2 us -> 0.64 us
  local copies, waits for them, and re-layouts: 1.55 us -> 8.73 us
  other arithmetic: 4.68 us -> 0 us
    pallas_call x0 -> x1, Pallas kernels: none -> 45.5 us  [body_fused(): pl.pallas_call(functools.partial(fused_kernel, steps, replicas, shards),...]
    dot_general x11 -> x0, matrix products: 36.5 us -> none  [the longest x1 13.7 us: body(): jnp.einsum('sbc,cd->sbd', attention_result, out_weight, preferred_element...]
    all_gather x5 -> x0, blocking collectives: 34.5 us -> none  [the longest x1 10.2 us: body(): lax.all_gather(down_qkv, 'replica', axis=2, tiled=True)]
    all_gather x1 -> x0, waiting for transfers between devices: 29.5 us -> none  [body(): output_up_complete = lax.all_gather(up_o_cols, 'tensor', axis=1, tiled=True)]
    psum x2 -> x0, blocking collectives: 27.8 us -> none  [the longest x1 19.2 us: body(): rank_sum = lax.psum(partial_rank, 'tensor')]
    psum x1 -> x0, waiting for transfers between devices: 15.4 us -> none  [body(): lax.psum((base_part, lowrank_portion), 'tensor')]
    unnamed x8 -> x4, local copies, waits for them, and re-layouts: 0.03 us -> 7.38 us
    convert_element_type x5 -> x0, other arithmetic: 1.92 us -> none  [the longest x1 0.99 us: body(): hidden_state = hidden.astype(jnp.float32)]
  transfers between devices with their start and end apart: 2 -> 0, of which waited for: 2 -> 0; matrix products, arithmetic and copies ran while one was open for 0% -> 0% of each run, Pallas kernels for 0% -> 0%
where the time goes in v1:
time: 55.2 us; the launch traced here: 54.9 us
  Pallas kernels  45.5 us (82%)
  local copies, waits for them, and re-layouts  8.73 us (16%)
  between operations  0.64 us (1%)
    pallas_call x1, Pallas kernels, body_fused(): pl.pallas_call(functools.partial(fused_kernel, steps, replicas, shards),...  45.5 us
    unnamed x4, local copies, waits for them, and re-layouts  7.38 us
    reshape x1, local copies, waits for them, and re-layouts, body_fused(): norm_gain.reshape(1, width)  1.35 us

profile of v1, /device:TPU:0, one launch (start us, length us, event | category | flops | bytes accessed | tf_op | source)
XLA Modules:
  0.0 54.9 jit_solution(8373725715571369142)
XLA Ops:
  0.6 1.4 %reshape.25.gain = bf16[1,8192]{1,0:T(2,128)(2,1)} reshape(bf16[8192]{0:T(1024)(128)(2,1)} %param.25) | data formatting | bytes 32768 | tf_op jit(solution)/shard_map/reshape | solution.py:617
  2.0 1.9 %copy.16.down_o_hbm = bf16[2048,16]{1,0:T(8,128)(2,1)} copy(bf16[2048,16]{0,1:T(8,128)(2,1)} %param.23) | data formatting | bytes 131072 | tf_op args[10]
  3.8 2.4 %copy.15.down_hbm = bf16[3,2048,16]{2,1,0:T(8,128)(2,1)} copy(bf16[3,2048,16]{1,2,0:T(8,128)(2,1)} %param.20) | data formatting | bytes 393216 | tf_op args[7]
  6.2 45.5 %shard_map.140 = (bf16[16,2048]{1,0:T(8,128)(2,1)}, bf16[16,8192]{1,0:T(8,128)(2,1)}) custom-call(bf16[16,8192]{1,0:T(8,128)(2,1)} %bitcast.5, bf16[16,2048]{1,0:T(8,128)(2,1)} %bitcast.8, bf16[2,16,1024]{2,1,0:T(8,128)(2,1)} %bitcast.9, s32[8]{0:T(128)} %lens.1, bf16[16,2048]{1,0:T(8,128)(2,1)} %up_q.1, bf16[2,16,1024]{2,1,0:T(8,128)(2,1)} %up_kv.1, ...), custom_call_target="tpu_custom_call" | custom-call | tf_op jit(solution)/shard_map/pallas_call | solution.py:562
  51.7 1.5 %copy.19 = bf16[2,8,2048]{2,1,0:T(8,128)(2,1)} copy(bf16[2,8,2048]{2,1,0:T(8,128)(2,1)} %bitcast.7) | data formatting | bytes 131072
  53.2 1.7 %copy.20 = bf16[2,8,8192]{2,1,0:T(8,128)(2,1)} copy(bf16[2,8,8192]{2,1,0:T(8,128)(2,1)} %bitcast.6) | data formatting | bytes 524288

commit v2 on v1

--- a/solution.py
+++ b/solution.py
@@ -157,14 +157,12 @@
     up_q,
     up_kv,
     up_o,
-    gain,
     down_hbm,
     down_o_hbm,
     keys_hbm,
     values_hbm,
     weight_hbm,
-    res_out,
-    norm_out,
+    full,
     keys,
     values,
     wbuf,
@@ -185,7 +183,6 @@
     sums_in,
     own,
     rank_out,
-    full,
     kv_sem,
     w_sem,
     down_sem,
@@ -277,31 +274,28 @@
             device_id_type=MESH,
         )
 
-    hid_mine = hid.at[:, pl.ds(pl.multiple_of(me_t * depth, 128), depth)]
+    state = hid[...].astype(jnp.float32)
+    scale = lax.rsqrt(jnp.mean(state * state, axis=-1, keepdims=True) + EPSILON)
+    hid_mine = hid[:, pl.ds(pl.multiple_of(me_t * depth, 128), depth)].astype(jnp.float32)
+    hid_all[0] = (hid_mine * scale).astype(jnp.bfloat16)
     kv_mine = up_kv.at[:, :, pl.ds(pl.multiple_of(me_t * kv_width, 128), kv_width)]
-    hid_copies = [to_replica(hid_mine, hid_all, 0, k) for k in range(1, replicas)]
+    hid_copies = [to_replica(hid_all.at[0], hid_all, 0, k) for k in range(1, replicas)]
     up_q_copies = [to_replica(up_q, up_q_all, 1, k) for k in range(1, replicas)]
     up_kv_copies = [to_replica(kv_mine, up_kv_all, 2, k) for k in range(1, replicas)]
     up_o_copies = [to_replica(up_o, up_o_all, 3, k) for k in range(1, replicas)]
     for copy in hid_copies + up_q_copies + up_kv_copies:
         copy.start()
-    hid_all[0] = hid_mine[...]
     up_q_all[0] = up_q[...]
     up_kv_all[0] = kv_mine[...]
     up_o_all[0] = up_o[...]
-
-    state = hid[...].astype(jnp.float32)
-    scale = lax.rsqrt(jnp.mean(state * state, axis=-1, keepdims=True) + EPSILON)
 
     down_copy.wait()
     for copy in hid_copies:
         copy.wait_recv()
     hid_rows = hid_all[...].reshape(replicas * tokens, depth)
-    pieces = [
-        jnp.dot(hid_rows, down[p], preferred_element_type=jnp.float32) for p in range(3)
-    ]
-    pieces.append(jnp.zeros((replicas * tokens, 128 - 3 * rank_share), jnp.float32))
-    part[...] = jnp.concatenate(pieces, axis=1).reshape(replicas, tokens, 128)
+    partial = dot_nt(hid_rows, down[...].reshape(3 * rank_share, depth))
+    blank = jnp.zeros((replicas * tokens, 128 - 3 * rank_share), jnp.float32)
+    part[...] = jnp.concatenate([partial, blank], axis=1).reshape(replicas, tokens, 128)
     part_copies = []
     for k in range(replicas):
         for m in range(shards):
@@ -324,16 +318,8 @@
     part_all[0, 0] = part[0]
 
     down_o_copy.wait()
-    eye = jnp.where(
-        lax.broadcasted_iota(jnp.int32, (rank_share, rank_share), 0)
-        == lax.broadcasted_iota(jnp.int32, (rank_share, rank_share), 1),
-        1.0,
-        0.0,
-    ).astype(jnp.bfloat16)
-    down_o_all[0] = dot_nt(eye, down_o[...]).astype(jnp.bfloat16)
-    down_o_copies = [
-        to_replica(down_o_all.at[0], down_o_all, 4, k) for k in range(1, replicas)
-    ]
+    down_o_all[0] = down_o[...]
+    down_o_copies = [to_replica(down_o, down_o_all, 4, k) for k in range(1, replicas)]
     for copy in down_o_copies + up_o_copies:
         copy.start()
 
@@ -344,7 +330,7 @@
         total = part_all[k, 0]
         for m in range(1, shards):
             total = total + part_all[k, m]
-        ranks.append((total * scale).astype(jnp.bfloat16))
+        ranks.append(total.astype(jnp.bfloat16))
 
     def rank_of(p):
         return jnp.concatenate(
@@ -491,7 +477,6 @@
             sum_copy(m, c).wait_recv()
             updated = updated + sums_in[m, c].astype(jnp.float32)
         rounded = updated.astype(jnp.bfloat16)
-        res_out[:, columns] = rounded
         full[me_t * chunks + c] = rounded
         for m in range(1, shards):
             full_copy(m, c).start()
@@ -505,16 +490,6 @@
     for c in range(chunks):
         for m in range(1, shards):
             arrived(m, c).wait_recv()
-    square = jnp.zeros((tokens, BLOCK), jnp.float32)
-    for i in range(shards * chunks):
-        block = full[i].astype(jnp.float32)
-        square = square + block * block
-    norm = lax.rsqrt(jnp.sum(square, axis=-1, keepdims=True) / width + EPSILON)
-    for i in range(shards * chunks):
-        columns = slice(i * BLOCK, (i + 1) * BLOCK)
-        norm_out[:, columns] = (
-            full[i].astype(jnp.float32) * norm * gain[:, columns].astype(jnp.float32)
-        ).astype(jnp.bfloat16)
 
     for copy in (
         hid_copies + up_q_copies + up_kv_copies + up_o_copies + down_o_copies + part_copies
@@ -526,6 +501,28 @@
         for c in range(chunks):
             sum_copy(m, c).wait_send()
             full_copy(m, c).wait_send()
+
+
+def norm_kernel(full, gain, res_out, norm_out):
+    blocks, tokens, block_width = full.shape
+    chunks = res_out.shape[1] // block_width
+    first = lax.axis_index("tensor") * chunks
+    for c in range(chunks):
+        res_out[:, c * block_width : (c + 1) * block_width] = full[first + c]
+    square = jnp.zeros((tokens, block_width), jnp.float32)
+    for i in range(blocks):
+        block = full[i].astype(jnp.float32)
+        square = square + block * block
+    mean = jnp.sum(square, axis=-1, keepdims=True) / (blocks * block_width)
+    norm = lax.rsqrt(mean + EPSILON)
+    gains = gain[...].astype(jnp.float32)
+    for i in range(blocks):
+        block = full[i].astype(jnp.float32) * norm
+        for j in range(0, block_width, 128):
+            line = (i * block_width + j) // 128
+            norm_out[:, i * block_width + j : i * block_width + j + 128] = (
+                block[:, j : j + 128] * gains[line : line + 1]
+            ).astype(jnp.bfloat16)
 
 
 def body_fused(
@@ -559,14 +556,13 @@
     bf16, f32 = jnp.bfloat16, jnp.float32
     dma = pltpu.SemaphoreType.DMA
     per_head = pltpu.VMEM((head_count, tokens, HD), f32)
-    residual, normed = pl.pallas_call(
+    down_qkv = jnp.swapaxes(down_qkv, 1, 2)
+    output_down_factor = output_down_factor.T
+    full = pl.pallas_call(
         functools.partial(fused_kernel, steps, replicas, shards),
-        out_shape=(
-            jax.ShapeDtypeStruct((tokens, share), bf16),
-            jax.ShapeDtypeStruct((tokens, width), bf16),
-        ),
-        in_specs=[vmem] * 3 + [smem] + [vmem] * 4 + [hbm] * 5,
-        out_specs=(vmem, vmem),
+        out_shape=jax.ShapeDtypeStruct((shards * chunks, tokens, BLOCK), bf16),
+        in_specs=[vmem] * 3 + [smem] + [vmem] * 3 + [hbm] * 5,
+        out_specs=vmem,
         scratch_shapes=[
             pltpu.VMEM(cache_keys.shape, bf16),
             pltpu.VMEM(cache_values.shape, bf16),
@@ -588,7 +584,6 @@
             pltpu.VMEM((shards, chunks, tokens, BLOCK), bf16),
             pltpu.VMEM((chunks, tokens, BLOCK), f32),
             pltpu.VMEM((shards, tokens, 128), f32),
-            pltpu.VMEM((shards * chunks, tokens, BLOCK), bf16),
             dma((2, rows)),
             dma((SLOTS,)),
             dma((2,)),
@@ -614,13 +609,21 @@
         query_up_factor,
         key_value_up_factor,
         output_up_factor,
-        norm_gain.reshape(1, width),
         down_qkv,
         output_down_factor,
         cache_keys,
         cache_values,
         out_weight,
     )
+    residual, normed = pl.pallas_call(
+        norm_kernel,
+        out_shape=(
+            jax.ShapeDtypeStruct((tokens, share), bf16),
+            jax.ShapeDtypeStruct((tokens, width), bf16),
+        ),
+        in_specs=[vmem, vmem],
+        out_specs=(vmem, vmem),
+    )(full, norm_gain.reshape(width // 128, 128))
     return residual.reshape(steps, rows, share), normed.reshape(steps, rows, width)
 
 

time: 55.2 us -> 47.9 us (0.87)
  local copies, waits for them, and re-layouts: 8.73 us -> 0 us
  Pallas kernels: 45.5 us -> 47.1 us
    unnamed x4 -> x0, local copies, waits for them, and re-layouts: 7.38 us -> none
    pallas_call x0 -> x1, Pallas kernels: none -> 1.84 us  [body_fused(): pl.pallas_call(norm_kernel, out_shape=(jax.ShapeDtypeStruct((tokens, shar...]
    reshape x1 -> x0, local copies, waits for them, and re-layouts: 1.35 us -> none  [body_fused(): norm_gain.reshape(1, width)]
where the time goes in v2:
time: 47.9 us; the launch traced here: 47.8 us
  Pallas kernels  47.1 us (98%)
  between operations  0.64 us (1%)
    pallas_call x1, Pallas kernels, body_fused(): pl.pallas_call(functools.partial(fused_kernel, steps, replicas, shards),...  45.3 us
    pallas_call x1, Pallas kernels, body_fused(): pl.pallas_call(norm_kernel, out_shape=(jax.ShapeDtypeStruct((tokens, shar...  1.84 us

profile of v2, /device:TPU:0, one launch (start us, length us, event | category | flops | bytes accessed | tf_op | source)
XLA Modules:
  0.0 47.8 jit_solution(670685779741911598)
XLA Ops:
  0.6 45.3 %shard_map.140.full = bf16[16,16,512]{2,1,0:T(8,128)(2,1)} custom-call(bf16[16,8192]{1,0:T(8,128)(2,1)} %bitcast.8, bf16[16,2048]{1,0:T(8,128)(2,1)} %bitcast.10, bf16[2,16,1024]{2,1,0:T(8,128)(2,1)} %bitcast.11, s32[8]{0:T(128)} %lens.1, bf16[16,2048]{1,0:T(8,128)(2,1)} %up_q.1, bf16[2,16,1024]{2,1,0:T(8,128)(2,1)} %up_kv.1, bf16[16,2048]{1,0:T(8,128)(2,1)} %up_o.1, ...), custom_call_target="tpu_custom_call" | custom-call | tf_op jit(solution)/shard_map/pallas_call | solution.py:561
  45.9 1.8 %shard_map.141 = (bf16[16,2048]{1,0:T(8,128)(2,1)}, bf16[16,8192]{1,0:T(8,128)(2,1)}) custom-call(bf16[16,16,512]{2,1,0:T(8,128)(2,1)} %shard_map.140.full, bf16[64,128]{1,0:T(8,128)(2,1)} %bitcast.13), custom_call_target="tpu_custom_call" | custom-call | tf_op jit(solution)/shard_map/pallas_call | solution.py:618

commit v3 on v2

--- a/solution.py
+++ b/solution.py
@@ -133,8 +133,9 @@
     return (residual_out, normed_out)
 
 
-BLOCK = 512
-SLOTS = 8
+BLOCK = 1024
+SLOTS = 4
+ROWS = 4
 MESH = pl.DeviceIdType.MESH
 
 
@@ -209,36 +210,6 @@
     kv_width = up_kv_all.shape[3]
     depth = hid_all.shape[2]
 
-    def key_copy(b):
-        return pltpu.make_async_copy(keys_hbm.at[b], keys.at[b], kv_sem.at[0, b])
-
-    def value_copy(b):
-        return pltpu.make_async_copy(values_hbm.at[b], values.at[b], kv_sem.at[1, b])
-
-    def weight_copy(m, c, slot):
-        column = pl.multiple_of(lax.rem(me_t + m, shards) * share + c * BLOCK, BLOCK)
-        return pltpu.make_async_copy(
-            weight_hbm.at[:, pl.ds(column, BLOCK)], wbuf.at[slot], w_sem.at[slot]
-        )
-
-    down_copy = pltpu.make_async_copy(down_hbm, down, down_sem.at[0])
-    down_o_copy = pltpu.make_async_copy(down_o_hbm, down_o, down_sem.at[1])
-    down_copy.start()
-    down_o_copy.start()
-
-    @pl.loop(0, rows)
-    def _(b):
-        key_copy(b).start()
-        value_copy(b).start()
-
-    order = [m % shards for m in range(1, shards + 1)]
-    held = SLOTS // chunks
-    for place in range(min(held, shards)):
-
-        @pl.loop(0, chunks)
-        def _(c, place=place):
-            weight_copy(order[place], c, place * chunks + c).start()
-
     barrier = pltpu.get_barrier_semaphore()
     for k in range(replicas):
         for m in range(shards):
@@ -252,6 +223,40 @@
                     },
                     device_id_type=MESH,
                 )
+    def key_copy(b):
+        return pltpu.make_async_copy(keys_hbm.at[b], keys.at[b], kv_sem.at[0, b])
+
+    def value_copy(b):
+        return pltpu.make_async_copy(values_hbm.at[b], values.at[b], kv_sem.at[1, b])
+
+    def weight_copy(m, c, slot):
+        column = pl.multiple_of(lax.rem(me_t + m, shards) * share + c * BLOCK, BLOCK)
+        return pltpu.make_async_copy(
+            weight_hbm.at[:, pl.ds(column, BLOCK)], wbuf.at[slot], w_sem.at[slot]
+        )
+
+    down_copy = pltpu.make_async_copy(down_hbm, down, down_sem.at[0])
+    down_o_copy = pltpu.make_async_copy(down_o_hbm, down_o, down_sem.at[1])
+    down_copy.start()
+    down_o_copy.start()
+
+    @pl.loop(0, rows)
+    def _(b):
+        key_copy(b).start()
+        value_copy(b).start()
+
+    order = [m % shards for m in range(1, shards + 1)]
+    held = SLOTS // chunks
+    for place in range(min(held, shards)):
+
+        @pl.loop(0, chunks)
+        def _(c, place=place):
+            weight_copy(order[place], c, place * chunks + c).start()
+
+    state = hid[...].astype(jnp.float32)
+    scale = lax.rsqrt(jnp.mean(state * state, axis=-1, keepdims=True) + EPSILON)
+    hid_mine = hid[:, pl.ds(pl.multiple_of(me_t * depth, 128), depth)].astype(jnp.float32)
+    hid_all[0] = (hid_mine * scale).astype(jnp.bfloat16)
     pl.semaphore_wait(barrier, replicas * shards - 1)
 
     def to_replica(src, dst, what, k):
@@ -274,10 +279,6 @@
             device_id_type=MESH,
         )
 
-    state = hid[...].astype(jnp.float32)
-    scale = lax.rsqrt(jnp.mean(state * state, axis=-1, keepdims=True) + EPSILON)
-    hid_mine = hid[:, pl.ds(pl.multiple_of(me_t * depth, 128), depth)].astype(jnp.float32)
-    hid_all[0] = (hid_mine * scale).astype(jnp.bfloat16)
     kv_mine = up_kv.at[:, :, pl.ds(pl.multiple_of(me_t * kv_width, 128), kv_width)]
     hid_copies = [to_replica(hid_all.at[0], hid_all, 0, k) for k in range(1, replicas)]
     up_q_copies = [to_replica(up_q, up_q_all, 1, k) for k in range(1, replicas)]
@@ -365,27 +366,27 @@
     place = lax.broadcasted_iota(jnp.int32, (lines, slots), 1)
     root = 1.0 / math.sqrt(HD)
 
-    @pl.loop(0, rows)
-    def _(b):
-        key_copy(b).wait()
-        value_copy(b).wait()
-
-        def line(source, s):
-            return source[:, pl.ds(s * rows + b, 1), :].reshape(heads, HD)
-
-        query = jnp.concatenate([line(q_heads, s) for s in range(steps)], axis=0)
-        scores = jnp.zeros((lines, slots), jnp.float32)
+    def line(source, s, b):
+        return source[:, pl.ds(s * rows + b, 1), :].reshape(heads, HD)
+
+    def score_row(b):
+        query = jnp.concatenate([line(q_heads, s, b) for s in range(steps)], axis=0)
+        scores = None
         for h in range(0, heads, 2):
             left = jnp.concatenate(
                 [jnp.where(line_head == h + i, query, 0.0) for i in range(2)], axis=1
             ).astype(jnp.bfloat16)
             pair = jnp.concatenate([keys[b, h], keys[b, h + 1]], axis=1)
-            scores = scores + dot_nt(left, pair)
+            product = dot_nt(left, pair)
+            scores = product if scores is None else scores + product
+        return query, scores
+
+    def weigh_row(b, query, scores):
         scores = jnp.where(place < lens[b], scores * root, NEG_FILL)
         highest = jnp.max(scores, axis=-1, keepdims=True)
         fresh_scores = []
         for t in range(steps):
-            new_key = jnp.concatenate([line(k_heads, t)] * steps, axis=0)
+            new_key = jnp.concatenate([line(k_heads, t, b)] * steps, axis=0)
             score = jnp.sum(query * new_key, axis=-1, keepdims=True) * root
             score = jnp.where(line_step >= t, score, NEG_FILL)
             fresh_scores.append(score)
@@ -399,9 +400,12 @@
         probs = (weights * inverse).astype(jnp.bfloat16)
         mixed = jnp.zeros((lines, HD), jnp.float32)
         for t in range(steps):
-            new_value = jnp.concatenate([line(v_heads, t)] * steps, axis=0)
+            new_value = jnp.concatenate([line(v_heads, t, b)] * steps, axis=0)
             prob = (fresh_exp[t] * inverse).astype(jnp.bfloat16).astype(jnp.float32)
             mixed = mixed + prob * new_value
+        return probs, mixed
+
+    def mix_row(b, probs, mixed):
         for h in range(0, heads, 2):
             pair = jnp.concatenate([values[b, h], values[b, h + 1]], axis=1)
             both = jnp.dot(probs, pair, preferred_element_type=jnp.float32)
@@ -413,6 +417,19 @@
             att_heads[:, pl.ds(s * rows + b, 1), :] = mixed[
                 s * heads : (s + 1) * heads
             ].reshape(heads, 1, HD)
+
+    together = math.gcd(rows, ROWS)
+
+    @pl.loop(0, rows, step=together)
+    def _(first):
+        batch = [first + i for i in range(together)]
+        for b in batch:
+            key_copy(b).wait()
+            value_copy(b).wait()
+        scored = [score_row(b) for b in batch]
+        weighed = [weigh_row(b, *of) for b, of in zip(batch, scored)]
+        for b, of in zip(batch, weighed):
+            mix_row(b, *of)
 
     attended = jnp.concatenate([att_heads[h] for h in range(heads)], axis=1).astype(jnp.bfloat16)
 

time: 47.9 us -> 44.7 us (0.933)
  Pallas kernels: 47.1 us -> 43.8 us
    pallas_call x1, Pallas kernels: 45.3 us -> 42 us  [body_fused(): pl.pallas_call(functools.partial(fused_kernel, steps, replicas, shards),...]
where the time goes in v3:
time: 44.7 us; the launch traced here: 44.5 us
  Pallas kernels  43.8 us (98%)
  between operations  0.64 us (1%)
    pallas_call x1, Pallas kernels, body_fused(): pl.pallas_call(functools.partial(fused_kernel, steps, replicas, shards),...  42 us
    pallas_call x1, Pallas kernels, body_fused(): pl.pallas_call(norm_kernel, out_shape=(jax.ShapeDtypeStruct((tokens, shar...  1.86 us

profile of v3, /device:TPU:0, one launch (start us, length us, event | category | flops | bytes accessed | tf_op | source)
XLA Modules:
  0.0 44.5 jit_solution(12767549748889211835)
XLA Ops:
  0.6 42.0 %shard_map.140.full = bf16[8,16,1024]{2,1,0:T(8,128)(2,1)} custom-call(bf16[16,8192]{1,0:T(8,128)(2,1)} %bitcast.8, bf16[16,2048]{1,0:T(8,128)(2,1)} %bitcast.10, bf16[2,16,1024]{2,1,0:T(8,128)(2,1)} %bitcast.11, s32[8]{0:T(128)} %lens.1, bf16[16,2048]{1,0:T(8,128)(2,1)} %up_q.1, bf16[2,16,1024]{2,1,0:T(8,128)(2,1)} %up_kv.1, bf16[16,2048]{1,0:T(8,128)(2,1)} %up_o.1, ...), custom_call_target="tpu_custom_call" | custom-call | tf_op jit(solution)/shard_map/pallas_call | solution.py:578
  42.6 1.9 %shard_map.141 = (bf16[16,2048]{1,0:T(8,128)(2,1)}, bf16[16,8192]{1,0:T(8,128)(2,1)}) custom-call(bf16[8,16,1024]{2,1,0:T(8,128)(2,1)} %shard_map.140.full, bf16[64,128]{1,0:T(8,128)(2,1)} %bitcast.13), custom_call_target="tpu_custom_call" | custom-call | tf_op jit(solution)/shard_map/pallas_call | solution.py:635
